TPU v7x, 128 devices: a whole 4x4x4 slice. The times are simulated.
128 devices in a mesh: mp: 8 (over z_lo, x), feat: 16 (over y, z_hi, core).
Axes of the slice: x: 4, y: 4, z: 4 (z_hi: 2, z_lo: 2; z = z_hi * 2 + z_lo), core: 2. Of those that a mesh axis runs over, the one named last changes fastest.
Arguments:
- residual_in: bfloat16 [256, 3584], P(None, 'feat'), may hold values from -24 to 24
- norm_gain: float32 [3584], P('feat'), may hold values from 0.5 to 1.5
- gate_weight: bfloat16 [3584, 14336], P('feat', 'mp'), may hold values from -0.09375 to 0.09375
- up_weight: bfloat16 [3584, 14336], P('feat', 'mp'), may hold values from -0.09375 to 0.09375
- down_weight: bfloat16 [14336, 3584], P('mp', 'feat'), may hold values from -0.046875 to 0.046875
- encoder_weight: bfloat16 [3584, 65536], P(None, ('mp', 'feat')), may hold values from -0.375 to 0.375
- encoder_bias: float32 [65536], P(('mp', 'feat')), may hold values from -1.5 to 0.5
- decoder_weight: bfloat16 [65536, 3584], P(('mp', 'feat')), may hold values from -0.09375 to 0.09375
- decoder_bias: float32 [3584], replicated, may hold values from -3 to 3
Outputs:
- feature_codes: bfloat16 [256, 65536], P(None, ('mp', 'feat'))
- reconstruction: bfloat16 [256, 3584], P(('mp', 'feat'))
- encoder_gradient: bfloat16 [3584, 65536], P(None, ('mp', 'feat'))
- decoder_gradient: bfloat16 [65536, 3584], P(('mp', 'feat'))
- input_gradient: float32 [256, 3584], P(('mp', 'feat'))
All inputs are finite; a program needn't handle non-finite values.
Results may differ from a plain program's by a relative error of at most 0.023.
Values may be sent and summed in bfloat16 or wider, within the bound.
No kernel may reach another device: no remote copies, remote signals or barrier semaphores. Data moves between devices by JAX's collectives and lax.ppermute only.
A program may use at most 128 MiB of HBM per device.

v0:
```python
import jax
import jax.numpy as jnp
from jax import lax
from jax.sharding import PartitionSpec as P

D = 3584
sparsity_weight = 0.2
norm_eps = 1e-06


def shards(
    residual_in,
    norm_gain,
    gate_weight,
    up_weight,
    down_weight,
    encoder_weight,
    encoder_bias,
    decoder_weight,
    decoder_bias,
):
    rows_all = residual_in.shape[0]
    hidden_local = gate_weight.shape[1]
    rows_own = rows_all // lax.axis_size(("mp", "feat"))
    first_row = lax.axis_index(("mp", "feat")) * rows_own
    source = residual_in.astype(jnp.float32)
    squares = lax.psum(jnp.sum(source * source, axis=1), "feat")
    inverse_scale = lax.rsqrt(squares / D + norm_eps)
    normed = (source * inverse_scale[:, None] * norm_gain[None, :]).astype(jnp.bfloat16)
    joint_weight = jnp.concatenate([gate_weight, up_weight], axis=1)
    row_block = normed
    projected = lax.psum_scatter(
        jnp.dot(row_block, joint_weight, preferred_element_type=jnp.float32).astype(jnp.bfloat16),
        "feat",
        scatter_dimension=0,
        tiled=True,
    ).astype(jnp.float32)
    hidden = (jax.nn.silu(projected[:, :hidden_local]) * projected[:, hidden_local:]).astype(
        jnp.bfloat16
    )
    partial_mixed = jnp.dot(
        lax.all_gather(hidden, "feat", axis=0, tiled=True),
        down_weight,
        preferred_element_type=jnp.float32,
    )
    mixed_terms = lax.psum(partial_mixed.astype(jnp.bfloat16), "mp").astype(jnp.float32)
    stream_cols = (source + mixed_terms).astype(jnp.bfloat16)
    stream = lax.all_gather(stream_cols, "feat", axis=1, tiled=True)
    encoded = (
        jnp.dot(stream, encoder_weight, preferred_element_type=jnp.float32) + encoder_bias[None, :]
    )
    feature_codes = jax.nn.softplus(encoded).astype(jnp.bfloat16)
    partial_recon = jnp.dot(feature_codes, decoder_weight, preferred_element_type=jnp.float32)
    summed = lax.psum(partial_recon, ("mp", "feat"))
    recon_all = summed + decoder_bias[None, :]
    error = (recon_all - stream.astype(jnp.float32)).astype(jnp.bfloat16)
    recon_own = lax.dynamic_slice_in_dim(recon_all, first_row, rows_own, 0)
    error_own = lax.dynamic_slice_in_dim(error, first_row, rows_own, 0)
    decoder_gradient = lax.dot_general(
        feature_codes, error, (((0,), (0,)), ((), ())), preferred_element_type=jnp.float32
    ).astype(jnp.bfloat16)
    code_gradient = lax.dot_general(
        error, decoder_weight, (((1,), (1,)), ((), ())), preferred_element_type=jnp.float32
    )
    encoded_gradient = (jax.nn.sigmoid(encoded) * (code_gradient + sparsity_weight)).astype(
        jnp.bfloat16
    )
    encoder_gradient = lax.dot_general(
        stream, encoded_gradient, (((0,), (0,)), ((), ())), preferred_element_type=jnp.float32
    ).astype(jnp.bfloat16)
    row_block = encoded_gradient
    input_gradient = lax.psum_scatter(
        lax.dot_general(
            row_block, encoder_weight, (((1,), (1,)), ((), ())), preferred_element_type=jnp.float32
        ),
        ("mp", "feat"),
        scatter_dimension=0,
        tiled=True,
    ) - error_own.astype(jnp.float32)
    return (
        feature_codes,
        recon_own.astype(jnp.bfloat16),
        encoder_gradient,
        decoder_gradient,
        input_gradient,
    )


def solution(mesh):
    in_specs = (
        P(None, "feat"),
        P("feat"),
        P("feat", "mp"),
        P("feat", "mp"),
        P("mp", "feat"),
        P(None, ("mp", "feat")),
        P(("mp", "feat")),
        P(("mp", "feat"), None),
        P(),
    )
    out_specs = (
        P(None, ("mp", "feat")),
        P(("mp", "feat"), None),
        P(None, ("mp", "feat")),
        P(("mp", "feat"), None),
        P(("mp", "feat"), None),
    )
    return jax.shard_map(shards, mesh=mesh, in_specs=in_specs, out_specs=out_specs, check_vma=False)
```

profile of v0, /device:TPU:1, one launch (start us, length us, event | category | flops | bytes accessed | tf_op | source)
XLA Modules:
  0.0 596.9 jit_solution(6068600141430006881)
XLA Ops:
  7.2 1.0 fusion.6
  8.2 35.1 %psum.21 = f32[256]{0:T(256)S(1)} all-reduce(f32[256]{0:T(256)S(1)} %fusion.6), channel_id=1, replica_groups=mesh['mp'=8,'feat'=16] {'feat'}, use_global_device_ids=true, to_apply=%region_1.0 | all-reduce | flops 256 | bytes 2048 | tf_op jit(solution)/shard_map/psum | solution.py:27
  43.3 3.5 convolution_convert_fusion.2
  46.9 69.5 %reduce-scatter.3.cloned.1.call-done = bf16[16,3584]{1,0:T(8,128)(2,1)} async-done(((bf16[256,3584]{1,0:T(8,128)(2,1)}), bf16[16,3584]{1,0:T(8,128)(2,1)}) %reduce-scatter.3.cloned.1.call-update) | async-done | bytes 114704 | tf_op jit(solution)/shard_map/reduce_scatter | solution.py:32
  116.4 0.9 convert_element_type.51
  117.3 26.6 %all_gather.6 = bf16[256,1792]{1,0:T(8,128)(2,1)S(1)} all-gather(bf16[16,1792]{1,0:T(8,128)(2,1)S(1)} %fusion.11), channel_id=1, replica_groups=mesh['mp'=8,'feat'=16] {'feat'}, dimensions={0}, use_global_device_ids=true | all-gather | bytes 974848 | tf_op jit(solution)/shard_map/all_gather | solution.py:42
  144.0 1.1 convolution_convert_fusion.3
  145.2 63.2 %all-reduce.5.cloned.1.call-done = bf16[256,224]{0,1:T(8,128)(2,1)} async-done(((bf16[256,224]{0,1:T(8,128)(2,1)}), bf16[256,224]{0,1:T(8,128)(2,1)}) %all-reduce.5.cloned.1.call-update) | async-done | bytes 114704 | tf_op jit(solution)/shard_map/psum | solution.py:46
  208.3 1.6 fusion.9
  210.0 55.2 %all-gather.2.cloned.1.call-done = bf16[256,3584]{0,1:T(8,128)(2,1)} async-done(((bf16[256,224]{0,1:T(8,128)(2,1)}), bf16[256,3584]{0,1:T(8,128)(2,1)}) %all-gather.2.cloned.1.call-update) | async-done | bytes 1835024 | tf_op jit(solution)/shard_map/all_gather | solution.py:48
  265.2 4.1 fusion.5
  270.0 3.5 fusion.15
  273.6 151.6 %all-reduce.7.cloned.1.call-done = f32[256,3584]{0,1:T(8,128)} async-done(((f32[256,3584]{0,1:T(8,128)}), f32[256,3584]{0,1:T(8,128)}) %all-reduce.7.cloned.1.call-update) | async-done | bytes 3670032 | tf_op jit(solution)/shard_map/psum | solution.py:54
  425.1 4.2 subtract_convert_fusion
  429.3 1.2 fusion.4
  431.3 0.8 copy-done.5
  432.1 3.0 fusion.16
  435.1 1.5 dynamic-slice_convert_fusion
  436.6 0.9 copy.20
  437.5 4.6 convolution_convert_fusion
  442.2 3.0 convolution_convert_fusion.1
  445.1 141.6 %all-reduce.9.cloned.1.call-done = f32[256,3584]{0,1:T(8,128)} async-done(((f32[256,3584]{0,1:T(8,128)}), f32[256,3584]{0,1:T(8,128)}) %all-reduce.9.cloned.1.call-update) | async-done | bytes 3670032
  586.7 2.5 dynamic-slice_subtract_fusion
  589.2 1.2 copy.21
  (35 shorter events, 1.9 us)
Async XLA Ops:
  7.2 136.8 %copy-start = (bf16[1792,224]{0,1:T(8,128)(2,1)S(1)}, bf16[1792,224]{0,1:T(8,128)(2,1)}, u32[]{:S(2)}) copy-start(bf16[1792,224]{0,1:T(8,128)(2,1)} %param.13) | copy-start | bytes 2408452
  7.2 109.2 %reduce-scatter.3.cloned.1.call-start = ((), (), s32[]{:S(2)}) async-start(), calls=%async_computation.1 | async-start | bytes 1949696 | tf_op jit(solution)/shard_map/reduce_scatter | solution.py:32
  43.3 165.0 %copy-start.9 = (bf16[256,224]{0,1:T(8,128)(2,1)S(1)}, bf16[256,224]{0,1:T(8,128)(2,1)}, u32[]{:S(2)}) copy-start(bf16[256,224]{0,1:T(8,128)(2,1)} %param.9) | copy-start | bytes 344068
  46.8 218.4 %copy-start.11 = (f32[512]{0:T(512)S(1)}, f32[512]{0:T(512)}, u32[]{:S(2)}) copy-start(f32[512]{0:T(512)} %param.15) | copy-start | bytes 6148
  46.8 161.5 %all-reduce.5.cloned.1.call-start = ((), (), s32[]{:S(2)}) async-start(), calls=%async_computation.2 | async-start | bytes 229376 | tf_op jit(solution)/shard_map/psum | solution.py:46
  145.1 120.1 %all-gather.2.cloned.1.call-start = ((), (), s32[]{:S(2)}) async-start(), calls=%async_computation.3 | async-start | bytes 1949696 | tf_op jit(solution)/shard_map/all_gather | solution.py:48
  209.9 215.2 %all-reduce.7.cloned.1.call-start = ((), (), s32[]{:S(2)}) async-start(), calls=%async_computation.4 | async-start | bytes 7340032 | tf_op jit(solution)/shard_map/psum | solution.py:54
  265.2 4.8 copy-start.3
  269.3 0.7 copy-start.6
  273.5 151.6 %copy-start.1 = (bf16[256,3584]{0,1:T(8,128)(2,1)S(1)}, bf16[256,3584]{0,1:T(8,128)(2,1)}, u32[]{:S(2)}) copy-start(bf16[256,3584]{0,1:T(8,128)(2,1)} %all-gather.2.cloned.1.call-done) | copy-start | bytes 5505028
  273.5 151.6 %copy-start.10 = (f32[3584]{0:T(1024)S(1)}, f32[3584]{0:T(1024)}, u32[]{:S(2)}) copy-start(f32[3584]{0:T(1024)} %param.17) | copy-start | bytes 43012
  273.5 313.2 %all-reduce.9.cloned.1.call-start = ((), (), s32[]{:S(2)}) async-start(), calls=%async_computation.5 | async-start | bytes 7340032
  425.1 4.2 copy-start.4
  429.3 1.3 copy-start.2
  429.3 2.8 copy-start.5
  430.6 0.7 copy-start.7
  437.5 4.6 copy-start.8
Sparse Core Ops, SparseCore 0:
  47.0 69.3 reduce-scatter.2
  145.3 63.0 all-reduce.4
  211.3 53.8 all-gather.1
  273.6 151.4 all-reduce.6
  435.2 151.4 all-reduce.8
where the time goes:
time: 597 us
  waiting for transfers between devices  481 us (81%)
  blocking collectives  61.7 us (10%)
  matrix products  23.9 us (4%)
  between operations  13.9 us (2%)
  other arithmetic  10.2 us (2%)
    psum x1, waiting for transfers between devices, shards(): summed = lax.psum(partial_recon, ('mp', 'feat'))  152 us
    unnamed x6, waiting for transfers between devices  142 us
    reduce_scatter x1, waiting for transfers between devices, shards(): lax.psum_scatter(jnp.dot(row_block, joint_weight, preferred_element_type=...  69.5 us
    psum x1, waiting for transfers between devices, shards(): lax.psum(partial_mixed.astype(jnp.bfloat16), 'mp').astype(jnp.float32)  63.2 us
    all_gather x1, waiting for transfers between devices, shards(): stream = lax.all_gather(stream_cols, 'feat', axis=1, tiled=True)  55.2 us
    psum x1, blocking collectives, shards(): squares = lax.psum(jnp.sum(source * source, axis=1), 'feat')  35.1 us
    all_gather x1, blocking collectives, shards(): lax.all_gather(hidden, 'feat', axis=0, tiled=True)  26.6 us
  transfers between devices with their start and end apart: 5, of which 5 were waited for; matrix products, arithmetic and copies ran while one was open for 2% of the time, Pallas kernels for 0%

commit v1 on v0

--- a/solution.py
+++ b/solution.py
@@ -6,6 +6,12 @@
 D = 3584
 sparsity_weight = 0.2
 norm_eps = 1e-06
+
+
+def gather_and_add(array, name):
+    parts = lax.all_gather(array, name, axis=0, tiled=False)
+    summed = parts.sum(axis=0)
+    return summed
 
 
 def shards(
@@ -43,7 +49,7 @@
         down_weight,
         preferred_element_type=jnp.float32,
     )
-    mixed_terms = lax.psum(partial_mixed.astype(jnp.bfloat16), "mp").astype(jnp.float32)
+    mixed_terms = gather_and_add(partial_mixed.astype(jnp.bfloat16), "mp").astype(jnp.float32)
     stream_cols = (source + mixed_terms).astype(jnp.bfloat16)
     stream = lax.all_gather(stream_cols, "feat", axis=1, tiled=True)
     encoded = (

time: 597 us -> 551 us (0.923)
  waiting for transfers between devices: 481 us -> 410 us
  blocking collectives: 61.7 us -> 86.5 us
    psum x1 -> x0, waiting for transfers between devices: 63.2 us -> none  [shards(): lax.psum(partial_mixed.astype(jnp.bfloat16), 'mp').astype(jnp.float32)]
    all_gather x0 -> x1, blocking collectives: none -> 24.7 us  [gather_and_add(): parts = lax.all_gather(array, name, axis=0, tiled=False)]
    unnamed x6 -> x5, waiting for transfers between devices: 142 us -> 143 us
  transfers between devices with their start and end apart: 5 -> 4, of which waited for: 5 -> 4; matrix products, arithmetic and copies ran while one was open for 2% -> 2% of each run, Pallas kernels for 0% -> 0%
where the time goes in v1:
time: 551 us; the launch traced here: 550 us
  waiting for transfers between devices  410 us (74%)
  blocking collectives  86.5 us (16%)
  matrix products  23.4 us (4%)
  between operations  13.9 us (3%)
  other arithmetic  9.47 us (2%)
  local copies, waits for them, and re-layouts  7.2 us (1%)
    psum x1, waiting for transfers between devices, shards(): summed = lax.psum(partial_recon, ('mp', 'feat'))  148 us
    unnamed x5, waiting for transfers between devices  143 us
    reduce_scatter x1, waiting for transfers between devices, shards(): lax.psum_scatter(jnp.dot(row_block, joint_weight, preferred_element_type=...  69.4 us
    all_gather x1, waiting for transfers between devices, shards(): stream = lax.all_gather(stream_cols, 'feat', axis=1, tiled=True)  49.9 us
    psum x1, blocking collectives, shards(): squares = lax.psum(jnp.sum(source * source, axis=1), 'feat')  35.1 us
    all_gather x1, blocking collectives, shards(): lax.all_gather(hidden, 'feat', axis=0, tiled=True)  26.7 us
    all_gather x1, blocking collectives, gather_and_add(): parts = lax.all_gather(array, name, axis=0, tiled=False)  24.7 us
  transfers between devices with their start and end apart: 4, of which 4 were waited for; matrix products, arithmetic and copies ran while one was open for 2% of the time, Pallas kernels for 0%

profile of v1, /device:TPU:1, one launch (start us, length us, event | category | flops | bytes accessed | tf_op | source)
XLA Modules:
  0.0 550.2 jit_solution(7885201123919470868)
XLA Ops:
  7.2 1.0 fusion.6
  8.2 35.1 %psum.14 = f32[256]{0:T(256)S(1)} all-reduce(f32[256]{0:T(256)S(1)} %fusion.6), channel_id=1, replica_groups=mesh['mp'=8,'feat'=16] {'feat'}, use_global_device_ids=true, to_apply=%region_1.0 | all-reduce | flops 256 | bytes 2048 | tf_op jit(solution)/shard_map/psum | solution.py:33
  43.3 3.4 convolution_convert_fusion.2
  46.9 69.4 %reduce-scatter.2.cloned.1.call-done = bf16[16,3584]{1,0:T(8,128)(2,1)} async-done(((bf16[256,3584]{1,0:T(8,128)(2,1)}), bf16[16,3584]{1,0:T(8,128)(2,1)}) %reduce-scatter.2.cloned.1.call-update) | async-done | bytes 114704 | tf_op jit(solution)/shard_map/reduce_scatter | solution.py:38
  116.3 0.9 convert_element_type.53
  117.3 26.7 %all_gather.12 = bf16[256,1792]{1,0:T(8,128)(2,1)S(1)} all-gather(bf16[16,1792]{1,0:T(8,128)(2,1)S(1)} %fusion.11), channel_id=1, replica_groups=mesh['mp'=8,'feat'=16] {'feat'}, dimensions={0}, use_global_device_ids=true | all-gather | bytes 974848 | tf_op jit(solution)/shard_map/all_gather | solution.py:48
  144.4 24.7 %all-gather = bf16[2048,224]{0,1:T(8,128)(2,1)S(1)} all-gather(bf16[256,224]{0,1:T(8,128)(2,1)S(1)} %convolution_convert_fusion.3), channel_id=2, replica_groups=mesh['mp'=8,'feat'=16] {'mp'}, dimensions={0}, use_global_device_ids=true | all-gather | bytes 1032192 | tf_op jit(solution)/shard_map/all_gather | solution.py:12
  169.4 0.7 bitcast_reduce_fusion
  170.1 0.7 fusion.9
  170.8 49.9 %all-gather.3.cloned.1.call-done = bf16[256,3584]{0,1:T(8,128)(2,1)} async-done(((bf16[256,224]{0,1:T(8,128)(2,1)}), bf16[256,3584]{0,1:T(8,128)(2,1)}) %all-gather.3.cloned.1.call-update) | async-done | bytes 1835024 | tf_op jit(solution)/shard_map/all_gather | solution.py:54
  220.7 4.9 fusion.5
  225.6 3.0 fusion.15
  228.6 1.4 copy-done.1
  230.0 2.5 copy.15
  232.6 147.5 %all-reduce.4.cloned.1.call-done = f32[256,3584]{1,0:T(8,128)} async-done(((f32[256,3584]{1,0:T(8,128)}), f32[256,3584]{1,0:T(8,128)}) %all-reduce.4.cloned.1.call-update) | async-done | bytes 3670032 | tf_op jit(solution)/shard_map/psum | solution.py:60
  380.1 4.6 subtract_convert_fusion
  384.8 1.2 fusion.4
  386.0 1.5 copy-done.5
  387.4 3.0 fusion.16
  390.5 4.5 convolution_convert_fusion
  395.0 3.0 convolution_convert_fusion.1
  398.0 1.4 dynamic-slice_convert_fusion
  399.4 142.7 %all-reduce.6.cloned.1.call-done = f32[256,3584]{1,0:T(8,128)} async-done(((f32[256,3584]{1,0:T(8,128)}), f32[256,3584]{1,0:T(8,128)}) %all-reduce.6.cloned.1.call-update) | async-done | bytes 3670032
  542.1 1.5 dynamic-slice_subtract_fusion
  (32 shorter events, 1.1 us)
Async XLA Ops:
  7.2 136.8 %copy-start = (bf16[1792,224]{0,1:T(8,128)(2,1)S(1)}, bf16[1792,224]{0,1:T(8,128)(2,1)}, u32[]{:S(2)}) copy-start(bf16[1792,224]{0,1:T(8,128)(2,1)} %param.13) | copy-start | bytes 2408452
  7.2 109.1 %reduce-scatter.2.cloned.1.call-start = ((), (), s32[]{:S(2)}) async-start(), calls=%async_computation.1 | async-start | bytes 1949696 | tf_op jit(solution)/shard_map/reduce_scatter | solution.py:38
  46.8 123.2 %copy-start.7 = (bf16[256,224]{0,1:T(8,128)(2,1)S(1)}, bf16[256,224]{0,1:T(8,128)(2,1)}, u32[]{:S(2)}) copy-start(bf16[256,224]{0,1:T(8,128)(2,1)} %param.9) | copy-start | bytes 344068
  46.8 173.8 %all-gather.3.cloned.1.call-start = ((), (), s32[]{:S(2)}) async-start(), calls=%async_computation.2 | async-start | bytes 1949696 | tf_op jit(solution)/shard_map/all_gather | solution.py:54
  117.2 103.5 %copy-start.9 = (f32[512]{0:T(512)S(1)}, f32[512]{0:T(512)}, u32[]{:S(2)}) copy-start(f32[512]{0:T(512)} %param.15) | copy-start | bytes 6148
  170.8 209.4 %all-reduce.4.cloned.1.call-start = ((), (), s32[]{:S(2)}) async-start(), calls=%async_computation.3 | async-start | bytes 7340032 | tf_op jit(solution)/shard_map/psum | solution.py:60
  220.7 4.9 copy-start.2
  225.5 165.0 %copy-start.6 = (bf16[256,512]{1,0:T(8,128)(2,1)}, bf16[256,512]{1,0:T(8,128)(2,1)S(1)}, u32[]{:S(2)}) copy-start(bf16[256,512]{1,0:T(8,128)(2,1)S(1)} %get-tuple-element.7) | copy-start | bytes 786436
  228.5 1.5 copy-start.1
  228.5 151.6 %copy-start.8 = (f32[3584]{0:T(1024)S(1)}, f32[3584]{0:T(1024)}, u32[]{:S(2)}) copy-start(f32[3584]{0:T(1024)} %param.17) | copy-start | bytes 43012
  228.6 313.5 %all-reduce.6.cloned.1.call-start = ((), (), s32[]{:S(2)}) async-start(), calls=%async_computation.4 | async-start | bytes 7340032
  380.1 4.6 copy-start.3
  380.1 4.6 copy-start.10
  384.7 1.2 copy-start.4
  384.7 2.7 copy-start.5
Sparse Core Ops, SparseCore 0:
  46.9 69.3 reduce-scatter.1
  170.9 49.7 all-gather.2
  228.7 151.4 all-reduce.3
  390.6 151.4 all-reduce.5
